TPU v7x, 256 devices: a whole 4x4x8 slice. The times are simulated.
256 devices in a mesh: gx: 4 (over y), gy: 4 (over x), gz: 16 (over z, core).
Axes of the slice: x: 4, y: 4, z: 8, core: 2. Of those that a mesh axis runs over, the one named last changes fastest.
Arguments:
- positions: float32 [3, 131072], P(None, ('gx', 'gy', 'gz')), may hold values from 0 to 8
- features: float32 [131072, 128], P(('gx', 'gy', 'gz')), may hold values from -6 to 6
- species: int32 [131072], P(('gx', 'gy', 'gz')), may hold values from 0 to 88
- species_embed: float32 [89, 128], replicated, may hold values from -3 to 3
- w_charge: float32 [128, 128], replicated, may hold values from -0.5 to 0.5
- wave_vectors: float32 [3, 1024], replicated, may hold values from -8 to 8
- wave_filter: float32 [1024, 128], replicated, may hold values from 0.02 to 0.2
- radial_decay: float32 [128], replicated, may hold values from 0.2 to 2
- w_edge: float32 [128, 128], replicated, may hold values from -0.5 to 0.5
- w_out: float32 [128, 128], replicated, may hold values from -0.5 to 0.5
- neighbour_index: int32 [131072, 16], P(('gx', 'gy', 'gz')), may hold values from 0 to 895
- edge_count: int32 [131072], P(('gx', 'gy', 'gz')), may hold values from 1 to 16
- edge_length: float32 [131072, 16], P(('gx', 'gy', 'gz')), may hold values from 0.8 to 4.5
- face_rows: int32 [1536, 64], P(('gx', 'gy', 'gz')), may hold values from 0 to 511
- cotangent: float32 [131072, 128], P(('gx', 'gy', 'gz')), may hold values from -6 to 6
Outputs:
- update: float32 [131072, 128], P(('gx', 'gy', 'gz'))
- grad_features: float32 [131072, 128], P(('gx', 'gy', 'gz'))
Inputs may be any that keep to these rules, and one draw needn't show every extreme that they name: `neighbour_index`: indexes the rows of the atom's brick's extended array: its 512 atoms, then six blocks of 64 received rows; slots at or past edge_count are unused. `face_rows`: rows 6 b to 6 b + 5 hold brick b's atoms (indices within the brick) sent to the lower and upper neighbours along gx, gy, gz in turn.
All inputs are finite; a program needn't handle non-finite values.
Results may differ from a plain program's by a relative error of at most 0.0003.
Values sent between devices are 32-bit elements; how exact they have to be, the bound alone decides.
A program may use at most 64 MiB of HBM per device.

v0:
```python
import jax
import jax.numpy as jnp
from jax import lax
from jax.sharding import PartitionSpec as P

cutoff = 5.0
highest = lax.Precision.HIGHEST


def padded_2(value, sides, width):
    for axis, dim in sides:
        devices, length = (lax.axis_size(axis), value.shape[dim])
        up = [(i, (i + 1) % devices) for i in range(devices)]
        down = [(j, i) for i, j in up]
        last = lax.slice_in_dim(value, length - width, length, axis=dim)
        leading = lax.slice_in_dim(value, 0, width, axis=dim)
        before = lax.ppermute(last, axis, up)
        after = lax.ppermute(leading, axis, down)
        value = jnp.concatenate([before, value, after], axis=dim)
    return value


def radial(edge_length, edge_count, radial_decay):
    scaled = edge_length / cutoff
    envelope = (1.0 - scaled * scaled) ** 2
    active = lax.broadcasted_iota(jnp.int32, edge_length.shape, 1) < edge_count[:, None]
    weight = jnp.where(active, envelope, 0.0)
    return weight[:, :, None] * jnp.exp(-radial_decay[None, None, :] * edge_length[:, :, None])


def contract(table, values):
    return lax.dot_general(table, values, (((0,), (0,)), ((), ())), precision=highest)


def across(outgoing, axis_id):
    if axis_id == 0:
        return padded_2(outgoing, (("gx", 0),), 1)
    if axis_id == 1:
        return padded_2(outgoing, (("gy", 0),), 1)
    return padded_2(outgoing, (("gz", 0),), 1)


def blocked(neighbour_index, edge_length, edge_count):
    atom_rows = neighbour_index.shape[0]
    block_rows = min(atom_rows, 256)
    block_count = atom_rows // block_rows
    return (
        neighbour_index.reshape(block_count, block_rows, -1),
        edge_length.reshape(block_count, block_rows, -1),
        edge_count.reshape(block_count, block_rows),
    )


def edge_sum(extended, neighbour_index, edge_length, edge_count, radial_decay):

    def block_sum(inputs):
        indices, lengths, counts = inputs
        weights = radial(lengths, counts, radial_decay)
        return jnp.sum(weights * extended[indices], axis=1)

    summed = lax.map(block_sum, blocked(neighbour_index, edge_length, edge_count))
    return summed.reshape(neighbour_index.shape[0], -1)


def edge_spread(grad_message, neighbour_index, edge_length, edge_count, radial_decay, ext_rows):
    indices, lengths, counts = blocked(neighbour_index, edge_length, edge_count)
    grad_blocks = grad_message.reshape(indices.shape[0], indices.shape[1], -1)

    def block_add(running, inputs):
        block_index, block_length, block_count, block_grad = inputs
        weights = radial(block_length, block_count, radial_decay)
        return (running.at[block_index].add(weights * block_grad[:, None, :]), None)

    start = jnp.zeros((ext_rows, grad_message.shape[1]), jnp.float32)
    return lax.scan(block_add, start, (indices, lengths, counts, grad_blocks))[0]


def per_device(
    positions,
    features,
    species,
    species_embed,
    w_charge,
    wave_vectors,
    wave_filter,
    radial_decay,
    w_edge,
    w_out,
    neighbour_index,
    edge_count,
    edge_length,
    face_rows,
    cotangent,
):
    atom_rows = features.shape[0]
    total_atoms = atom_rows * lax.axis_size("gx") * lax.axis_size("gy") * lax.axis_size("gz")
    scaling = total_atoms ** (-0.5)
    onehot = (
        species[:, None] == lax.broadcasted_iota(jnp.int32, (1, species_embed.shape[0]), 1)
    ).astype(jnp.float32)
    charges = jnp.dot(features, w_charge, precision=highest) + jnp.dot(
        onehot, species_embed, precision=highest
    )
    phases = lax.dot_general(wave_vectors, positions, (((0,), (0,)), ((), ())), precision=highest)
    cosines = jnp.cos(phases)
    sines = jnp.sin(phases)
    partial_value = (
        jnp.stack(
            [
                jnp.dot(cosines, charges, precision=highest),
                jnp.dot(sines, charges, precision=highest),
            ]
        )
        * scaling
    )
    structure = lax.psum(partial_value, ("gx", "gy", "gz"))
    filtered = wave_filter[None] * structure
    received = [features]
    for axis_id in range(3):
        outgoing = jnp.stack(
            [features[face_rows[2 * axis_id]], features[face_rows[2 * axis_id + 1]]]
        )
        padded = across(outgoing, axis_id)
        received.append(padded[0])
        received.append(padded[3])
    extended = jnp.concatenate(received, axis=0)
    messages = edge_sum(extended, neighbour_index, edge_length, edge_count, radial_decay)
    potential = contract(cosines, filtered[0]) + contract(sines, filtered[1])
    preact = jnp.dot(potential, w_out, precision=highest) + jnp.dot(
        messages, w_edge, precision=highest
    )
    gate_value = jax.nn.sigmoid(preact)
    update = preact * gate_value
    grad_preact = cotangent * gate_value * (1.0 + preact * (1.0 - gate_value))
    grad_potential = jnp.dot(grad_preact, w_out.T, precision=highest)
    grad_message = jnp.dot(grad_preact, w_edge.T, precision=highest)
    back_term = jnp.stack(
        [
            jnp.dot(cosines, grad_potential, precision=highest),
            jnp.dot(sines, grad_potential, precision=highest),
        ]
    )
    back_total = lax.psum(back_term, ("gx", "gy", "gz"))
    grad_structure = wave_filter[None] * back_total
    grad_extended = edge_spread(
        grad_message, neighbour_index, edge_length, edge_count, radial_decay, extended.shape[0]
    )
    grad_charges = (
        contract(cosines, grad_structure[0]) + contract(sines, grad_structure[1])
    ) * scaling
    gradient = grad_extended[:atom_rows] + jnp.dot(grad_charges, w_charge.T, precision=highest)
    halo_rows = face_rows.shape[1]
    returned = grad_extended[atom_rows:].reshape(6, halo_rows, -1)
    for axis_id in range(3):
        outgoing = jnp.stack([returned[2 * axis_id], returned[2 * axis_id + 1]])
        padded = across(outgoing, axis_id)
        gradient = gradient.at[face_rows[2 * axis_id]].add(padded[0])
        gradient = gradient.at[face_rows[2 * axis_id + 1]].add(padded[3])
    return (update, gradient)


def solution(mesh):
    in_specs = (
        P(None, ("gx", "gy", "gz")),
        P(("gx", "gy", "gz"), None),
        P(("gx", "gy", "gz")),
        P(),
        P(),
        P(),
        P(),
        P(),
        P(),
        P(),
        P(("gx", "gy", "gz"), None),
        P(("gx", "gy", "gz")),
        P(("gx", "gy", "gz"), None),
        P(("gx", "gy", "gz"), None),
        P(("gx", "gy", "gz"), None),
    )
    out_specs = (P(("gx", "gy", "gz"), None), P(("gx", "gy", "gz"), None))
    return jax.shard_map(
        per_device, mesh=mesh, in_specs=in_specs, out_specs=out_specs, check_vma=False
    )
```

profile of v0, /device:TPU:1, one launch (start us, length us, event | category | flops | bytes accessed | tf_op | source)
XLA Modules:
  0.0 594.2 jit_solution(5919708666812183825)
XLA Ops:
  8.2 1.6 gather_fusion.1
  9.8 2.2 collective-permute-start
  12.0 1.5 gather_fusion.2
  13.5 1.5 collective-permute-start.1
  15.0 1.5 gather_fusion.3
  17.9 1.5 gather_fusion.4
  19.4 2.0 collective-permute-start.3
  21.4 1.5 gather_fusion.5
  23.0 3.3 collective-permute-start.4
  26.3 9.6 %fusion.26 = (f32[1024,512]{1,0:T(8,128)S(1)}, f32[1024,512]{1,0:T(8,128)S(1)}) fusion(f32[3,1024]{1,0:T(4,128)} %param.24, f32[3,512]{1,0:T(4,128)} %param.19), kind=kOutput, calls=%fused_computation.101 | convolution fusion | flops 18874368 | bytes 4212736 | tf_op jit(solution)/shard_map/dot_general | solution.py:104
  36.7 1.8 convolution_bitcast_fusion.2
  38.5 2.0 convolution_bitcast_fusion.3
  43.1 3.0 collective-permute-done.5
  46.1 26.7 %while.24 = (s32[]{:T(128)}, f32[2,256,128]{2,1,0:T(8,128)}, s32[2,256]{1,0:T(2,128)S(1)}, f32[2,256,16]{2,1,0:T(8,128)S(1)}, f32[1,1,128]{2,1,0:T(1,128)S(1)}, ...) while((s32[]{:T(128)}, f32[2,256,128]{2,1,0:T(8,128)}, s32[2,256]{1,0:T(2,128)S(1)}, ...), condition=%wide.region_3.4_spmd, body=%wide.region_1.3_spmd.sunk | while | flops 2105346 | bytes 6885473 | solution.py:61
  46.3 10.8 %gather_fusion = f32[4096,128]{1,0:T(8,128)S(1)} fusion(f32[896,128]{1,0:T(8,128)S(1)} %get-tuple-element.355, s32[4096]{0:T(1024)S(1)} %broadcast_clamp_fusion.2), kind=kCustom, calls=%fused_computation.clone.1 | custom fusion | bytes 4210688 | tf_op jit(solution)/shard_map/while/body/eval_jaxpr/gather | solution.py:59
  57.1 1.6 multiply_reduce_fusion.2
  59.7 10.8 %gather_fusion = f32[4096,128]{1,0:T(8,128)S(1)} fusion(f32[896,128]{1,0:T(8,128)S(1)} %get-tuple-element.355, s32[4096]{0:T(1024)S(1)} %broadcast_clamp_fusion.2), kind=kCustom, calls=%fused_computation.clone.1 | custom fusion | bytes 4210688 | tf_op jit(solution)/shard_map/while/body/eval_jaxpr/gather | solution.py:59
  70.5 1.6 multiply_reduce_fusion.2
  72.8 222.8 %all-reduce.3.cloned.1.call-done = f32[2,1024,128]{2,1,0:T(8,128)} async-done(((f32[2,1024,128]{2,1,0:T(8,128)}), f32[2,1024,128]{2,1,0:T(8,128)}) %all-reduce.3.cloned.1.call-update) | async-done | bytes 1048592 | tf_op jit(solution)/shard_map/psum | solution.py:116
  297.0 3.4 fusion.2
  300.5 3.4 convolution_add_fusion.3
  304.3 2.0 fusion.3
  306.8 1.8 convolution_bitcast_fusion.1
  308.6 1.8 convolution_bitcast_fusion
  312.2 48.2 %while.25 = (s32[]{:T(128)}, f32[896,128]{1,0:T(8,128)S(1)}, s32[2,256,16]{2,1,0:T(8,128)S(1)}, s32[2,256]{1,0:T(2,128)S(1)}, f32[2,256,16]{2,1,0:T(8,128)S(1)},...) while((s32[]{:T(128)}, f32[896,128]{1,0:T(8,128)S(1)}, s32[2,256,16]{2,1,0:T(8,128)S(1)}, ...), condition=%wide.region_6.7_spmd, body=%wide.region_4.6_spmd.sunk | while | flops 2134018 | bytes 8969941 | solution.py:75
  313.7 22.6 %scatter_fusion = f32[896,128]{1,0:T(8,128)S(1)} fusion(f32[896,128]{1,0:T(8,128)S(1)} %get-tuple-element.366, s32[4096]{0:T(1024)S(1)} %reshape.492, f32[4096,128]{1,0:T(8,128)S(1)} %bitcast.168), kind=kCustom, calls=%fused_computation.7.clone.1 | custom fusion | flops 524288 | bytes 6307840 | tf_op jit(solution)/shard_map/while/body/eval_jaxpr/scatter-add | solution.py:72
  337.8 22.6 %scatter_fusion = f32[896,128]{1,0:T(8,128)S(1)} fusion(f32[896,128]{1,0:T(8,128)S(1)} %get-tuple-element.366, s32[4096]{0:T(1024)S(1)} %reshape.492, f32[4096,128]{1,0:T(8,128)S(1)} %bitcast.168), kind=kCustom, calls=%fused_computation.7.clone.1 | custom fusion | flops 524288 | bytes 6307840 | tf_op jit(solution)/shard_map/while/body/eval_jaxpr/scatter-add | solution.py:72
  365.8 2.2 collective-permute-start.10
  368.0 198.9 %all-reduce.5.cloned.1.call-done = f32[2,1024,128]{2,1,0:T(8,128)} async-done(((f32[2,1024,128]{2,1,0:T(8,128)}), f32[2,1024,128]{2,1,0:T(8,128)}) %all-reduce.5.cloned.1.call-update) | async-done | bytes 1048592 | tf_op jit(solution)/shard_map/psum | solution.py:143
  568.4 5.0 fusion.1
  573.5 3.4 fusion
  576.9 2.1 collective-permute-start.11
  (144 shorter events, 28.9 us)
Async XLA Ops:
  7.2 297.1 %copy-start = (f32[128,128]{1,0:T(8,128)S(1)}, f32[128,128]{1,0:T(8,128)}, u32[]{:S(2)}) copy-start(f32[128,128]{1,0:T(8,128)} %param.27) | copy-start | bytes 196612
  7.2 288.4 %all-reduce.3.cloned.1.call-start = ((), (), s32[]{:S(2)}) async-start(), calls=%async_computation | async-start | bytes 2097152 | tf_op jit(solution)/shard_map/psum | solution.py:116
  8.1 6.9 %copy-start.22 = (s32[64]{0:T(128)}, s32[64]{0:T(128)S(1)}, u32[]{:S(2)}) copy-start(s32[64]{0:T(128)S(1)} %get-tuple-element.225) | copy-start | bytes 772
  8.1 13.3 %copy-start.21 = (s32[64]{0:T(128)}, s32[64]{0:T(128)S(1)}, u32[]{:S(2)}) copy-start(s32[64]{0:T(128)S(1)} %get-tuple-element.226) | copy-start | bytes 772
  8.2 14.8 %copy-start.23 = (s32[64]{0:T(128)}, s32[64]{0:T(128)S(1)}, u32[]{:S(2)}) copy-start(s32[64]{0:T(128)S(1)} %get-tuple-element.228) | copy-start | bytes 772
  8.2 14.8 %copy-start.24 = (s32[64]{0:T(128)}, s32[64]{0:T(128)S(1)}, u32[]{:S(2)}) copy-start(s32[64]{0:T(128)S(1)} %get-tuple-element.227) | copy-start | bytes 772
  8.2 27.8 %copy-start.19 = (s32[64]{0:T(128)}, s32[64]{0:T(128)S(1)}, u32[]{:S(2)}) copy-start(s32[64]{0:T(128)S(1)} %get-tuple-element.229) | copy-start | bytes 772
  8.2 27.8 %copy-start.20 = (s32[64]{0:T(128)}, s32[64]{0:T(128)S(1)}, u32[]{:S(2)}) copy-start(s32[64]{0:T(128)S(1)} %get-tuple-element.224) | copy-start | bytes 772
  9.8 32.9 %collective-permute-start = (f32[1,64,128]{2,1,0:T(8,128)S(1)}, f32[1,64,128]{2,1,0:T(8,128)S(1)}, u32[]{:S(2)}, u32[]{:S(2)}) collective-permute-start(f32[1,64,128]{2,1,0:T(8,128)S(1)} %bitcast.179), channel_id=1, source_target_pairs={{0,64},{64,128},{128,192},{192,0},{1,65},{65,129},{129,193},{193,1... | collective-permute-start | bytes 98312 | tf_op jit(solution)/shard_map/ppermute | solution.py:17
  13.5 29.5 %collective-permute-start.1 = (f32[1,64,128]{2,1,0:T(8,128)S(1)}, f32[1,64,128]{2,1,0:T(8,128)S(1)}, u32[]{:S(2)}, u32[]{:S(2)}) collective-permute-start(f32[1,64,128]{2,1,0:T(8,128)S(1)} %bitcast.176), channel_id=1, source_target_pairs={{64,0},{128,64},{192,128},{0,192},{65,1},{129,65},{193,129},{1,193... | collective-permute-start | bytes 98312 | tf_op jit(solution)/shard_map/ppermute | solution.py:18
  16.6 26.4 %collective-permute-start.2 = (f32[1,64,128]{2,1,0:T(8,128)S(1)}, f32[1,64,128]{2,1,0:T(8,128)S(1)}, u32[]{:S(2)}, u32[]{:S(2)}) collective-permute-start(f32[1,64,128]{2,1,0:T(8,128)S(1)} %bitcast.177), channel_id=1, source_target_pairs={{0,16},{16,32},{32,48},{48,0},{1,17},{17,33},{33,49},{49,1},{2,18}... | collective-permute-start | bytes 98312 | tf_op jit(solution)/shard_map/ppermute | solution.py:17
  19.4 23.6 %collective-permute-start.3 = (f32[1,64,128]{2,1,0:T(8,128)S(1)}, f32[1,64,128]{2,1,0:T(8,128)S(1)}, u32[]{:S(2)}, u32[]{:S(2)}) collective-permute-start(f32[1,64,128]{2,1,0:T(8,128)S(1)} %bitcast.178), channel_id=1, source_target_pairs={{16,0},{32,16},{48,32},{0,48},{17,1},{33,17},{49,33},{1,49},{18,2}... | collective-permute-start | bytes 98312 | tf_op jit(solution)/shard_map/ppermute | solution.py:18
  23.0 13.0 %copy-start.15 = (f32[89,128]{1,0:T(8,128)S(1)}, f32[89,128]{1,0:T(8,128)}, u32[]{:S(2)}) copy-start(f32[89,128]{1,0:T(8,128)} %param.22) | copy-start | bytes 136708
  23.0 13.0 %copy-start.18 = (s32[512]{0:T(512)S(1)}, s32[512]{0:T(512)}, u32[]{:S(2)}) copy-start(s32[512]{0:T(512)} %param.21) | copy-start | bytes 6148
  23.0 13.3 %copy-start.6 = (f32[512,128]{1,0:T(8,128)S(1)}, f32[512,128]{1,0:T(8,128)}, u32[]{:S(2)}) copy-start(f32[512,128]{1,0:T(8,128)} %param.20) | copy-start | bytes 786436
  23.0 13.3 %copy-start.8 = (f32[128,128]{1,0:T(8,128)S(1)}, f32[128,128]{1,0:T(8,128)}, u32[]{:S(2)}) copy-start(f32[128,128]{1,0:T(8,128)} %param.23) | copy-start | bytes 196612
  23.0 20.0 %collective-permute-start.4 = (f32[1,64,128]{2,1,0:T(8,128)S(1)}, f32[1,64,128]{2,1,0:T(8,128)S(1)}, u32[]{:S(2)}, u32[]{:S(2)}) collective-permute-start(f32[1,64,128]{2,1,0:T(8,128)S(1)} %bitcast.180), channel_id=1, source_target_pairs={{0,1},{1,2},{2,3},{3,4},{4,5},{5,6},{6,7},{7,8},{8,9},{9,10},{10,1... | collective-permute-start | bytes 98312 | tf_op jit(solution)/shard_map/ppermute | solution.py:17
  41.7 525.3 %all-reduce.5.cloned.1.call-start = ((), (), s32[]{:S(2)}) async-start(), calls=%async_computation.1 | async-start | bytes 2097152 | tf_op jit(solution)/shard_map/psum | solution.py:143
  42.7 3.4 collective-permute-start.5
  72.8 224.2 %copy-start.5 = (f32[1024,512]{1,0:T(8,128)S(1)}, f32[1024,512]{1,0:T(8,128)}, u32[]{:S(2)}) copy-start(f32[1024,512]{1,0:T(8,128)} %copy-done.4) | copy-start | bytes 6291460
  300.5 5.9 copy-start.26
  313.7 22.6 %copy-start.11 = (s32[2,256]{1,0:T(2,128)S(1)}, s32[2,256]{1,0:T(2,128)}, u32[]{:S(2)}) copy-start(s32[2,256]{1,0:T(2,128)} %copy-done.10) | copy-start | bytes 6148 | tf_op jit(solution)/shard_map/while
  313.7 22.6 %copy-start.14 = (f32[1,1,128]{2,1,0:T(1,128)S(1)}, f32[1,1,128]{2,1,0:T(1,128)}, u32[]{:S(2)}) copy-start(f32[1,1,128]{2,1,0:T(1,128)} %copy-done.13) | copy-start | bytes 1540 | tf_op jit(solution)/shard_map/while
  337.8 22.6 %copy-start.11 = (s32[2,256]{1,0:T(2,128)S(1)}, s32[2,256]{1,0:T(2,128)}, u32[]{:S(2)}) copy-start(s32[2,256]{1,0:T(2,128)} %copy-done.10) | copy-start | bytes 6148 | tf_op jit(solution)/shard_map/while
  337.8 22.6 %copy-start.14 = (f32[1,1,128]{2,1,0:T(1,128)S(1)}, f32[1,1,128]{2,1,0:T(1,128)}, u32[]{:S(2)}) copy-start(f32[1,1,128]{2,1,0:T(1,128)} %copy-done.13) | copy-start | bytes 1540 | tf_op jit(solution)/shard_map/while
  360.4 216.5 %collective-permute-start.6 = (f32[1,64,128]{2,1,0:T(8,128)S(1)}, f32[1,64,128]{2,1,0:T(8,128)S(1)}, u32[]{:S(2)}, u32[]{:S(2)}) collective-permute-start(f32[1,64,128]{2,1,0:T(8,128)S(1)} %get-tuple-element.223), channel_id=1, source_target_pairs={{0,64},{64,128},{128,192},{192,0},{1,65},{65,129},{129,193},{193,1... | collective-permute-start | bytes 98312 | tf_op jit(solution)/shard_map/ppermute | solution.py:17
  361.7 218.9 %collective-permute-start.7 = (f32[1,64,128]{2,1,0:T(8,128)S(1)}, f32[1,64,128]{2,1,0:T(8,128)S(1)}, u32[]{:S(2)}, u32[]{:S(2)}) collective-permute-start(f32[1,64,128]{2,1,0:T(8,128)S(1)} %get-tuple-element.222), channel_id=1, source_target_pairs={{64,0},{128,64},{192,128},{0,192},{65,1},{129,65},{193,129},{1,193... | collective-permute-start | bytes 98312 | tf_op jit(solution)/shard_map/ppermute | solution.py:18
  363.1 218.6 %collective-permute-start.8 = (f32[1,64,128]{2,1,0:T(8,128)S(1)}, f32[1,64,128]{2,1,0:T(8,128)S(1)}, u32[]{:S(2)}, u32[]{:S(2)}) collective-permute-start(f32[1,64,128]{2,1,0:T(8,128)S(1)} %get-tuple-element.221), channel_id=1, source_target_pairs={{0,16},{16,32},{32,48},{48,0},{1,17},{17,33},{33,49},{49,1},{2,18}... | collective-permute-start | bytes 98312 | tf_op jit(solution)/shard_map/ppermute | solution.py:17
  364.3 218.6 %collective-permute-start.9 = (f32[1,64,128]{2,1,0:T(8,128)S(1)}, f32[1,64,128]{2,1,0:T(8,128)S(1)}, u32[]{:S(2)}, u32[]{:S(2)}) collective-permute-start(f32[1,64,128]{2,1,0:T(8,128)S(1)} %get-tuple-element.220), channel_id=1, source_target_pairs={{16,0},{32,16},{48,32},{0,48},{17,1},{33,17},{49,33},{1,49},{18,2}... | collective-permute-start | bytes 98312 | tf_op jit(solution)/shard_map/ppermute | solution.py:18
  365.8 207.6 %copy-start.3 = (f32[1024,512]{1,0:T(8,128)S(1)}, f32[1024,512]{1,0:T(8,128)}, u32[]{:S(2)}) copy-start(f32[1024,512]{1,0:T(8,128)} %copy-done.1) | copy-start | bytes 6291460
  365.8 218.3 %collective-permute-start.10 = (f32[1,64,128]{2,1,0:T(8,128)S(1)}, f32[1,64,128]{2,1,0:T(8,128)S(1)}, u32[]{:S(2)}, u32[]{:S(2)}) collective-permute-start(f32[1,64,128]{2,1,0:T(8,128)S(1)} %get-tuple-element.219), channel_id=1, source_target_pairs={{0,1},{1,2},{2,3},{3,4},{4,5},{5,6},{6,7},{7,8},{8,9},{9,10},{10,1... | collective-permute-start | bytes 98312 | tf_op jit(solution)/shard_map/ppermute | solution.py:17
  576.9 8.3 %collective-permute-start.11 = (f32[1,64,128]{2,1,0:T(8,128)S(1)}, f32[1,64,128]{2,1,0:T(8,128)S(1)}, u32[]{:S(2)}, u32[]{:S(2)}) collective-permute-start(f32[1,64,128]{2,1,0:T(8,128)S(1)} %get-tuple-element.218), channel_id=1, source_target_pairs={{1,0},{2,1},{3,2},{4,3},{5,4},{6,5},{7,6},{8,7},{9,8},{10,9},{11,1... | collective-permute-start | bytes 98312 | tf_op jit(solution)/shard_map/ppermute | solution.py:18
  (14 other events, 34.6 us)
Sparse Core Ops, SparseCore 0:
  41.8 253.6 all-reduce.2
  312.2 254.6 all-reduce.4
where the time goes:
time: 598 us; the launch traced here: 594 us
  waiting for transfers between devices  425 us (71%)
  other arithmetic  64 us (11%)
  matrix products  36.8 us (6%)
  local copies, waits for them, and re-layouts  32.9 us (6%)
  starting transfers between devices  20.4 us (3%)
  between operations  14.9 us (2%)
    psum x1, waiting for transfers between devices, per_device(): structure = lax.psum(partial_value, ('gx', 'gy', 'gz'))  223 us
    psum x1, waiting for transfers between devices, per_device(): back_total = lax.psum(back_term, ('gx', 'gy', 'gz'))  199 us
    scatter-add x2, other arithmetic, block_add(): return (running.at[block_index].add(weights * block_grad[:, None, :]), None)  45.1 us
    gather x2, local copies, waits for them, and re-layouts, block_sum(): return jnp.sum(weights * extended[indices], axis=1)  21.5 us
    dot_general x4, matrix products, contract(): lax.dot_general(table, values, (((0,), (0,)), ((), ())), precision=highest)  15.3 us
  transfers between devices with their start and end apart: 14, of which 3 were waited for; matrix products, arithmetic and copies ran while one was open for 19% of the time, Pallas kernels for 0%

commit v1 on v0

v1 whole, which is shorter than its diff:
```python
import functools
import math

import jax
import jax.numpy as jnp
from jax import lax
from jax.experimental import pallas as pl
from jax.experimental.pallas import tpu as pltpu
from jax.sharding import PartitionSpec as P

f32, bf16 = jnp.float32, jnp.bfloat16
MESH = pl.DeviceIdType.MESH
AXES = ("gx", "gy", "gz")
NX, NY, NZ = 4, 4, 16
XY = NX * NY
ZC = NZ // 2
A = 512
C = 128
KH = 512
ROWS = 2 * KH
PART = ROWS // XY
GROUP = ROWS // NX
HALO = 64
EXT = A + 6 * HALO
NB = 16
SPECIES = 89
CUTOFF = 5.0
SCALE = float((A * NX * NY * NZ) ** -0.5)
LOG2E = math.log2(math.e)
MAGIC = 12582912.0
SIN = (6.2831828185508565, -41.34142139866063, 81.59618387211225, -76.5801005149952, 41.20539481223465, -12.271262263060988)
COS = (0.9999999891722592, -19.739204532088973, 64.93911898363098, -85.45016554576007, 60.16783169583647, -25.968313174868474, 6.529610245007803)
ORDER = (2, 1, 3, 0)


def split(x):
    hi = x.astype(bf16)
    return hi, (x - hi.astype(f32)).astype(bf16)


def pair(x, axis=1):
    return jnp.concatenate(split(x), axis=axis)


def dot(a, b, dims=((1,), (0,))):
    return lax.dot_general(a, b, (dims, ((), ())), preferred_element_type=f32)


def fold(r):
    return r[:, :C] + r[:, C:]


def dot3(a_hi, a_lo, b_pair):
    return fold(dot(a_hi, b_pair)) + dot(a_lo, b_pair[:, :C])


def mm3(a, b):
    return dot3(*split(a), pair(b))


def mm3_nt(a, b):
    hi, lo = split(a)
    b_pair = pair(b, 0)
    r = dot(hi, b_pair, ((1,), (1,)))
    n = b.shape[0]
    return r[:, :n] + r[:, n:] + dot(lo, b_pair[:n], ((1,), (1,)))


def turns(ph):
    r = ph - ((ph + MAGIC) - MAGIC)
    u = r * r
    s, c = jnp.full_like(u, SIN[-1]), jnp.full_like(u, COS[-1])
    for k in SIN[-2::-1]:
        s = s * u + k
    for k in COS[-2::-1]:
        c = c * u + k
    return c, s * r


def kernel(
    pos_ref, feat_ref, spec_ref, emb_ref, wch_ref, wave_ref, filt_ref, decay_ref, wedge_ref, wout_ref,
    idx_ref, cnt_ref, len_ref, face_ref, cot_ref,
    upd_ref, grad_ref,
    pos_own, pos_in, q, pst, wst, wstt, ph, thi, tlo, tthi, ttlo,
    struct, rs, zs, zb, full, pacc, pout, pin, gp, back, rs2, zs2, zb2, full2, pacc2, pout2, pin2,
    emb_pad, facerow, oface, feat_t, extt, halo_out, halo_in, back_out, back_in,
    idx_t, len_t, env_t, dec_t, rad, msg, msgw, gmt, ge, gmain,
    send, recv, group_recv,
):
    gx, gy, gz = (lax.axis_index(a) for a in AXES)
    core = lax.rem(gz, 2)
    xy = gx * NY + gy
    partner = (gx, gy, gz + 1 - 2 * core)

    def shifted(dx, dy, dz):
        return (lax.rem(gx + dx, NX), lax.rem(gy + dy, NY), lax.rem(gz + dz, NZ))

    far_z = (gx, gy, lax.rem(gz + NZ - 1 + 2 * core, NZ))
    peers = [shifted(dx, dy, 0) for dx in range(NX) for dy in range(NY) if dx or dy]
    peers += [shifted(0, 0, 2 * dz) for dz in range(1, ZC)]
    peers += [partner, far_z]
    barrier = pltpu.get_barrier_semaphore()
    for peer in peers:
        pl.semaphore_signal(barrier, inc=1, device_id=peer, device_id_type=MESH)

    def copy(src, dst, send_id, recv_sem, device):
        return pltpu.make_async_remote_copy(
            src_ref=src, dst_ref=dst, send_sem=send.at[send_id], recv_sem=recv_sem, device_id=device, device_id_type=MESH
        )

    def arrived(ref, sem):
        copy(ref, ref, 0, sem, partner).wait_recv()

    def left(ref, send_id):
        copy(ref, ref, send_id, recv.at[0], partner).wait_send()

    feat = feat_ref[...]
    emb_pad[...] = jnp.zeros_like(emb_pad)
    emb_pad[0:SPECIES, :] = emb_ref[...]
    of_species = (lax.broadcasted_iota(jnp.int32, (C, A), 0) == spec_ref[...]).astype(f32).astype(bf16)
    q[0] = mm3(feat, wch_ref[...]) + fold(dot(of_species, pair(emb_pad[...]), ((0,), (0,))))

    def parts(x):
        p1 = x.astype(bf16).astype(f32)
        p2 = (x - p1).astype(bf16).astype(f32)
        return p1, p2, ((x - p1) - p2).astype(bf16).astype(f32)

    pos_own[...] = jnp.zeros_like(pos_own)
    pos_own[0:3, :] = pos_ref[...] * (1.0 / (2.0 * math.pi))
    wst[...] = jnp.zeros_like(wst)
    wparts = parts(wave_ref[:, pl.ds(pl.multiple_of(core * KH, KH), KH)])
    for i, k in enumerate((0, 0, 1, 1, 0, 2)):
        wst[8 * i : 8 * i + 3, :] = wparts[k]
    wstt[...] = wst[...].T

    def set_positions(half, value):
        pparts = parts(value)
        for i, k in enumerate((0, 1, 0, 1, 2, 0)):
            pst[8 * i : 8 * i + 8, A * half : A * half + A] = pparts[k]

    def tables(g, half):
        cols = slice(A * half, A * half + A)
        krow = pl.multiple_of(g * (GROUP // 2), GROUP // 2)
        ph[...] = dot(wstt[pl.ds(krow, GROUP // 2), :].astype(bf16), pst[:, cols].astype(bf16))
        row = pl.multiple_of(g * GROUP, GROUP)
        for i in range(4):
            c, s = turns(ph[32 * i : 32 * i + 32, :])
            for j, x in enumerate((c, s)):
                hi, lo = split(x)
                at = pl.ds(row + 64 * i + 32 * j, 32)
                thi[at, cols] = hi
                tlo[at, cols] = lo

    set_positions(0, pos_own[...])

    def own_tables(g, _):
        tables(g, 0)
        return 0

    lax.fori_loop(0, NX, own_tables, 0)

    pl.semaphore_wait(barrier, len(peers))
    copy(q.at[0], q.at[1], 0, recv.at[0], partner).start()
    copy(pos_own, pos_in, 1, recv.at[1], partner).start()

    for i in range(6):
        facerow[0:1, HALO * i : HALO * i + HALO] = face_ref[i : i + 1, :]
    oface[...] = (lax.broadcasted_iota(jnp.int32, (A, 6 * HALO), 0) == facerow[0:1, :]).astype(f32).astype(bf16)
    halo_out[...] = fold(dot(oface[...], pair(feat), ((0,), (0,))))

    def exchange_faces(src, dst, send_id, recv_id, slot):
        for t, (lower, upper) in enumerate((
            (shifted(NX - 1, 0, 0), shifted(1, 0, 0)),
            (shifted(0, NY - 1, 0), shifted(0, 1, 0)),
            (shifted(0, 0, NZ - 1), shifted(0, 0, 1)),
        )):
            for side, device in ((0, lower), (1, upper)):
                out, there = 2 * t + side, 2 * t + 1 - side
                copy(
                    src.at[pl.ds(slot + HALO * out, HALO)], dst.at[pl.ds(HALO * there, HALO)], send_id, recv.at[recv_id], device
                ).start()

    exchange_faces(halo_out, halo_in, 2, 2, 0)

    arrived(pos_in, recv.at[1])
    set_positions(1, pos_in[...])
    arrived(q.at[1], recv.at[0])
    q_pair = jnp.concatenate([pair(q[0]), pair(q[1])], axis=0)

    def rows(g):
        return pl.ds(pl.multiple_of(g * GROUP, GROUP), GROUP)

    def scatter_group(dx, src, dst, send_id, recv_id):
        for dy in ORDER:
            if dx or dy:
                device = shifted(dx, dy, 0)
                p = device[0] * NY + device[1]
                copy(
                    src.at[pl.ds(pl.multiple_of(p * PART, PART), PART)], dst.at[dx * NY + dy], send_id, recv.at[recv_id], device
                ).start()

    for dx in ORDER:
        g = lax.rem(gx + dx, NX)
        tables(g, 1)
        struct[rows(g), :] = dot3(thi[rows(g), :], tlo[rows(g), :], q_pair)
        scatter_group(dx, struct, rs, 3, 3)

    def mine(src):
        return src[pl.ds(pl.multiple_of(xy * PART, PART), PART), :]

    def along_z(total, zs, zb, send_id, recv_id):
        zs[...] = total
        for dz in (4, 3, 5, 2, 6, 1, 7):
            copy(zs, zb.at[dz], send_id, recv.at[recv_id], shifted(0, 0, 2 * dz)).start()

    def gather_parts(value, full, send_id, sems):
        own = full.at[pl.ds(pl.multiple_of(xy * PART, PART), PART)]
        own[...] = value
        for dx in ORDER:
            for dy in ORDER:
                if dx or dy:
                    copy(own, own, send_id, group_recv.at[sems + dx], shifted(dx, dy, 0)).start()

    def group_arrived(dx, full, sems):
        g = lax.rem(gx + NX - dx, NX)
        n = GROUP if dx else GROUP - PART
        arrived(full.at[pl.ds(0, n)], group_recv.at[sems + dx])
        return g

    def transposed(g, _):
        tthi[g] = thi[rows(g), :].T
        ttlo[g] = tlo[rows(g), :].T
        return 0

    lax.fori_loop(0, NX, transposed, 0)
    idx_t[...] = idx_ref[...].T
    length = len_ref[...].T
    len_t[...] = length
    scaled = length * (1.0 / CUTOFF)
    envelope = 1.0 - scaled * scaled
    live = lax.broadcasted_iota(jnp.int32, (NB, A), 0) < cnt_ref[...]
    env_t[...] = jnp.where(live, envelope * envelope, 0.0)
    dec_t[...] = jnp.broadcast_to(decay_ref[...] * (-LOG2E), (C, C)).T
    extt[:, 0:A] = pair(feat_ref[...].T, 0)

    def one_hot(e):
        return (lax.broadcasted_iota(jnp.int32, (EXT, A), 0) == idx_t[pl.ds(e, 1), :]).astype(f32).astype(bf16)

    def gather_edge(e, _):
        got = dot(extt[...], one_hot(e))
        decay = jnp.concatenate([dec_t[...]] * 4, axis=1)
        radial = env_t[pl.ds(e, 1), :] * jnp.exp2(decay * len_t[pl.ds(e, 1), :])
        rad[e] = radial
        msg[...] += radial * (got[:C] + got[C:])
        return 0

    arrived(halo_in, recv.at[2])
    extt[:, A:EXT] = pair(halo_in[...].T, 0)
    msg[...] = jnp.zeros_like(msg)

    arrived(rs.at[pl.ds(1, XY - 1)], recv.at[3])
    total = mine(struct)
    for i in range(1, XY):
        total = total + rs[i]
    along_z(total, zs, zb, 4, 4)

    lax.fori_loop(0, NB // 2, gather_edge, 0)

    arrived(zb.at[pl.ds(1, ZC - 1)], recv.at[4])
    filt = filt_ref[pl.ds(pl.multiple_of(core * KH + xy * (PART // 2), PART // 2), PART // 2), :]
    filt = jnp.concatenate([filt, filt], axis=0) * SCALE
    total = zs[...]
    for i in range(1, ZC):
        total = total + zb[i]
    gather_parts(mm3(total * filt, wout_ref[...]), full, 5, 0)

    lax.fori_loop(NB // 2, NB, gather_edge, 0)
    msgw[...] = mm3(msg[...].T, wedge_ref[...])

    def spread_parts(full, sems, pacc, pout, pin, send_id, recv_id):
        pacc[...] = jnp.zeros_like(pacc)
        for dx in (0, 1, 3):
            g = group_arrived(dx, full, sems)
            pacc[...] += dot3(tthi[g], ttlo[g], pair(full[rows(g), :]))
        g = group_arrived(2, full, sems)
        f_pair = pair(full[rows(g), :])
        pout[...] = pacc[A:, :] + dot3(tthi[g, A:], ttlo[g, A:], f_pair)
        copy(pout, pin, send_id, recv.at[recv_id], partner).start()
        mine = pacc[:A, :] + dot3(tthi[g, :A], ttlo[g, :A], f_pair)
        arrived(pin, recv.at[recv_id])
        return mine + pin[...]

    preact = spread_parts(full, 0, pacc, pout, pin, 6, 5) + msgw[...]
    gate = jax.nn.sigmoid(preact)
    upd_ref[...] = preact * gate
    gp[0] = cot_ref[...] * gate * (1.0 + preact * (1.0 - gate))
    copy(gp.at[0], gp.at[1], 7, recv.at[6], partner).start()

    gp_pair = pair(gp[0])
    back[...] = dot3(thi[:, :A], tlo[:, :A], gp_pair)
    arrived(gp.at[1], recv.at[6])
    gp_pair = pair(gp[1])
    for dx in ORDER:
        g = lax.rem(gx + dx, NX)
        back[rows(g), :] += dot3(thi[rows(g), A:], tlo[rows(g), A:], gp_pair)
        scatter_group(dx, back, rs2, 8, 7)

    gmt[...] = mm3_nt(wedge_ref[...], gp[0])
    ge[...] = jnp.zeros_like(ge)

    def spread_edge(e, _):
        ge[...] += dot(one_hot(e), pair(rad[e] * gmt[...], 0), ((1,), (1,)))
        return 0

    lax.fori_loop(0, NB // 2, spread_edge, 0)

    arrived(rs2.at[pl.ds(1, XY - 1)], recv.at[7])
    total = mine(back)
    for i in range(1, XY):
        total = total + rs2[i]
    along_z(total, zs2, zb2, 9, 8)

    lax.fori_loop(NB // 2, NB, spread_edge, 0)
    back_out[...] = fold(ge[A:, :])
    exchange_faces(back_out, back_in, 10, 9, 0)

    arrived(zb2.at[pl.ds(1, ZC - 1)], recv.at[8])
    total = zs2[...]
    for i in range(1, ZC):
        total = total + zb2[i]
    value = mm3_nt(mm3_nt(total, wout_ref[...]) * filt, wch_ref[...])
    gather_parts(value, full2, 11, 4)

    arrived(back_in, recv.at[9])
    gmain[...] = fold(ge[:A, :]) + fold(dot(oface[...], pair(back_in[...])))
    grad_ref[...] = spread_parts(full2, 4, pacc2, pout2, pin2, 12, 10) + gmain[...]

    for ref, i in (
        (q.at[0], 0), (pos_own, 1), (halo_out, 2), (rs.at[pl.ds(1, XY - 1)], 3), (zb.at[pl.ds(1, ZC - 1)], 4),
        (rs.at[pl.ds(1, XY - 1)], 5), (pout, 6), (gp.at[0], 7), (rs.at[pl.ds(1, XY - 1)], 8), (zb.at[pl.ds(1, ZC - 1)], 9),
        (halo_out, 10), (rs.at[pl.ds(1, XY - 1)], 11), (pout, 12),
    ):
        left(ref, i)


def per_device(
    positions, features, species, species_embed, w_charge, wave_vectors, wave_filter, radial_decay, w_edge, w_out,
    neighbour_index, edge_count, edge_length, face_rows, cotangent,
):
    v = lambda *shape: pltpu.VMEM(shape, f32)
    h = lambda *shape: pltpu.VMEM(shape, bf16)
    reduction = [v(ROWS, C), v(XY, PART, C), v(PART, C), v(ZC, PART, C), v(ROWS, C), v(2 * A, C), v(A, C), v(A, C)]
    scratch = [
        v(8, A), v(8, A), v(2, A, C), v(48, 2 * A), v(48, KH), v(KH, 48), v(GROUP // 2, A),
        h(ROWS, 2 * A), h(ROWS, 2 * A), h(NX, 2 * A, GROUP), h(NX, 2 * A, GROUP),
        *reduction, v(2, A, C), *reduction,
        v(C, C), pltpu.VMEM((8, 6 * HALO), jnp.int32), h(A, 6 * HALO), v(8, C), h(2 * C, EXT),
        v(6 * HALO, C), v(6 * HALO, C), v(6 * HALO, C), v(6 * HALO, C),
        pltpu.VMEM((NB, A), jnp.int32), v(NB, A), v(NB, A), v(C, C), v(NB, C, A), v(C, A), v(A, C), v(C, A),
        v(EXT, 2 * C), v(A, C),
        pltpu.SemaphoreType.DMA((13,)), pltpu.SemaphoreType.DMA((11,)), pltpu.SemaphoreType.DMA((8,)),
    ]
    shape = jax.ShapeDtypeStruct((A, C), f32)
    vmem = pl.BlockSpec(memory_space=pltpu.VMEM)
    return pl.pallas_call(
        kernel,
        out_shape=(shape, shape),
        in_specs=[vmem] * 15,
        out_specs=(vmem, vmem),
        scratch_shapes=scratch,
        compiler_params=pltpu.CompilerParams(collective_id=0, has_side_effects=True, vmem_limit_bytes=60 << 20),
        name="block",
    )(
        positions, features, species.reshape(1, A), species_embed, w_charge, wave_vectors, wave_filter,
        radial_decay.reshape(1, C), w_edge, w_out, neighbour_index, edge_count.reshape(1, A), edge_length, face_rows, cotangent,
    )


def solution(mesh):
    atoms = P(AXES, None)
    row = P(AXES)
    in_specs = (P(None, AXES), atoms, row, P(), P(), P(), P(), P(), P(), P(), atoms, row, atoms, atoms, atoms)
    return jax.shard_map(per_device, mesh=mesh, in_specs=in_specs, out_specs=(atoms, atoms), check_vma=False)
```

time: 598 us -> 76.2 us (0.13)
  waiting for transfers between devices: 425 us -> 0 us
  Pallas kernels: 0 us -> 70.5 us
  other arithmetic: 64 us -> 0 us
  matrix products: 36.8 us -> 0 us
  local copies, waits for them, and re-layouts: 32.9 us -> 4.86 us
  starting transfers between devices: 20.4 us -> 0 us
  between operations: 14.9 us -> 0.66 us
    psum x2 -> x0, waiting for transfers between devices: 422 us -> none  [the longest x1 223 us: per_device(): structure = lax.psum(partial_value, ('gx', 'gy', 'gz'))]
    pallas_call x0 -> x1, Pallas kernels: none -> 70.5 us  [per_device(): pl.pallas_call(kernel, out_shape=(shape, shape), in_specs=[vmem] * 15, ou...]
    scatter-add x8 -> x0, other arithmetic: 52 us -> none  [the longest x2 45.1 us: block_add(): return (running.at[block_index].add(weights * block_grad[:, None, :]), None)]
    dot_general x16 -> x0, matrix products: 36.8 us -> none  [the longest x4 15.3 us: contract(): lax.dot_general(table, values, (((0,), (0,)), ((), ())), precision=highest)]
    gather x8 -> x0, local copies, waits for them, and re-layouts: 29.9 us -> none  [the longest x2 21.5 us: block_sum(): return jnp.sum(weights * extended[indices], axis=1)]
    ppermute x12 -> x0, starting transfers between devices: 20.3 us -> none  [the longest x6 11.4 us: padded_2(): before = lax.ppermute(last, axis, up)]
    mul x5 -> x0, other arithmetic: 6.25 us -> none  [the longest x2 2.29 us: block_add(): return (running.at[block_index].add(weights * block_grad[:, None, :]), None)]
  transfers between devices with their start and end apart: 14 -> 0, of which waited for: 3 -> 0; matrix products, arithmetic and copies ran while one was open for 19% -> 0% of each run, Pallas kernels for 0% -> 0%
where the time goes in v1:
time: 76.2 us; the launch traced here: 76 us
  Pallas kernels  70.5 us (93%)
  local copies, waits for them, and re-layouts  4.86 us (6%)
    pallas_call x1, Pallas kernels, per_device(): pl.pallas_call(kernel, out_shape=(shape, shape), in_specs=[vmem] * 15, ou...  70.5 us
    unnamed x8, local copies, waits for them, and re-layouts  4.86 us

profile of v1, /device:TPU:1, one launch (start us, length us, event | category | flops | bytes accessed | tf_op | source)
XLA Modules:
  0.0 76.0 jit_solution(12740529039834714892)
XLA Ops:
  0.6 0.0 copy-start.1
  0.6 1.6 %copy.17.idx_ref = s32[512,16]{1,0:T(8,128)} copy(s32[512,16]{0,1:T(8,128)} %param.25) | data formatting | bytes 65536 | tf_op args[10]
  2.2 0.0 copy-done.1
  2.2 0.8 %copy.18.len_ref = f32[512,16]{1,0:T(8,128)} copy(f32[512,16]{0,1:T(8,128)S(1)} %copy-done.1) | data formatting | bytes 65536 | tf_op args[12]
  3.1 70.5 %block.1 = (f32[512,128]{1,0:T(8,128)}, f32[512,128]{1,0:T(8,128)}) custom-call(f32[3,512]{1,0:T(4,128)} %pos_ref.1, f32[512,128]{1,0:T(8,128)} %feat_ref.1, s32[1,512]{1,0:T(1,128)} %bitcast.3, f32[89,128]{1,0:T(8,128)} %emb_ref.1, f32[128,128]{1,0:T(8,128)} %wch_ref.1, f32[3,1024]{1,0:T(4,128)} %wave_ref.1, f32[1024,128]{1,0:T(8,128)} %filt_ref.1, ...), custom_call_target="tpu_custom_call" | custom-call | tf_op jit(solution)/shard_map/block/pallas_call | solution.py:365
  73.6 0.0 copy-start
  73.6 1.7 %copy.21 = f32[512,128]{1,0:T(8,128)} copy(f32[512,128]{1,0:T(8,128)} %get-tuple-element.4) | data formatting | bytes 524288
  75.3 0.0 copy-done
  75.3 0.7 copy.22
Async XLA Ops:
  0.6 1.6 %copy-start.1 = (f32[512,16]{0,1:T(8,128)S(1)}, f32[512,16]{0,1:T(8,128)}, u32[]{:S(2)}) copy-start(f32[512,16]{0,1:T(8,128)} %param.27) | copy-start | bytes 98308
  73.6 1.7 %copy-start = (f32[512,128]{1,0:T(8,128)S(1)}, f32[512,128]{1,0:T(8,128)}, u32[]{:S(2)}) copy-start(f32[512,128]{1,0:T(8,128)} %get-tuple-element.5) | copy-start | bytes 786436
